TPU v7x, 256 devices: a whole 4x4x8 slice. The times are simulated.
256 devices in a mesh: rows: 16 (over z, core), group: 16 (over x, y).
Axes of the slice: x: 4, y: 4, z: 8, core: 2. Of those that a mesh axis runs over, the one named last changes fastest.
Arguments:
- embeddings: bfloat16 [65536, 256], P(('rows', 'group')), may hold values from -6 to 6
- fine_labels: int32 [65536], P(('rows', 'group')), may hold values from 0 to 16383
- prototypes: bfloat16 [16384, 256], P('group'), may hold values from -2.25 to 2.25
- coarse_protos: bfloat16 [1024, 256], replicated, may hold values from -0.190625 to 0.190625
- coarse_labels: int32 [16384], P('group'), may hold values from 0 to 1023
Outputs:
- grad_embeddings: float32 [65536, 256], P(('rows', 'group'))
- grad_prototypes: float32 [16384, 256], P('group')
- new_prototypes: float32 [16384, 256], P('group')
- grad_coarse: float32 [1024, 256], replicated
- total_loss: float32 [], replicated
All inputs are finite; a program needn't handle non-finite values.
Results may differ from a plain program's by a relative error of at most 0.007.
Values may be sent and summed in bfloat16 or wider, within the bound.
A program may use at most 64 MiB of HBM per device.

v0:
```python
import jax
import jax.numpy as jnp
from jax import lax
from jax.sharding import PartitionSpec as P


def body(embeddings, fine_labels, prototypes, coarse_protos, coarse_labels):
    groups = lax.axis_size("group")
    group_index = lax.axis_index("group")
    row_devices = lax.axis_size("rows")
    row_index = lax.axis_index("rows")
    own_rows = embeddings.shape[0]
    feature_dim = embeddings.shape[1]
    local_k = prototypes.shape[0]
    coarse_count = coarse_protos.shape[0]
    total_rows = own_rows * row_devices * groups
    total_k = local_k * groups
    emb_float = embeddings.astype(jnp.float32)
    inverse = lax.rsqrt(jnp.sum(emb_float * emb_float, axis=1, keepdims=True) + 1e-06)
    unit_rows = emb_float * inverse
    unit_half = unit_rows.astype(jnp.bfloat16)
    gathered = lax.all_gather(unit_half, "group", axis=0, tiled=True)
    gathered_labels = lax.all_gather(fine_labels, "group", axis=0, tiled=True)
    local_labels = gathered_labels - group_index * local_k
    gathered_rows = gathered.shape[0]
    block_rows = min(512, gathered_rows)
    nblock = gathered_rows // block_rows
    row_blocks = gathered.reshape(nblock, block_rows, feature_dim)
    label_blocks = local_labels.reshape(nblock, block_rows)
    columns = jnp.arange(local_k, dtype=jnp.int32)

    def scores(rows_half):
        return 10.0 * lax.dot_general(
            rows_half, prototypes, (((1,), (1,)), ((), ())), preferred_element_type=jnp.float32
        )

    def stats_block(inputs):
        rows_half, labels = inputs
        logits = scores(rows_half)
        largest = jnp.max(logits, axis=1)
        expsum = jnp.sum(jnp.exp(logits - largest[:, None]), axis=1)
        target = jnp.sum(jnp.where(columns[None, :] == labels[:, None], logits, 0.0), axis=1)
        return (largest, expsum, target)

    row_peak, row_total, row_target = lax.map(stats_block, (row_blocks, label_blocks))
    row_peak = row_peak.reshape(gathered_rows)
    row_total = row_total.reshape(gathered_rows)
    row_target = row_target.reshape(gathered_rows)
    global_peak = lax.pmax(row_peak, "group")
    global_total, global_target = lax.psum(
        (row_total * jnp.exp(row_peak - global_peak), row_target), "group"
    )
    log_total = global_peak + jnp.log(global_total)
    mine = lax.dynamic_slice_in_dim(log_total - global_target, group_index * own_rows, own_rows, 0)
    fine_loss = jnp.sum(mine)
    total_blocks = log_total.reshape(nblock, block_rows)

    def grads_block(running, inputs):
        grad_proto, member_sum = running
        rows_half, labels, totals = inputs
        logits = scores(rows_half)
        member = columns[None, :] == labels[:, None]
        delta = (10.0 * (jnp.exp(logits - totals[:, None]) - member.astype(jnp.float32))).astype(
            jnp.bfloat16
        )
        row_terms = jnp.dot(delta, prototypes, preferred_element_type=jnp.float32)
        grad_proto = grad_proto + lax.dot_general(
            delta, rows_half, (((0,), (0,)), ((), ())), preferred_element_type=jnp.float32
        )
        member_sum = member_sum + lax.dot_general(
            member.astype(jnp.bfloat16),
            rows_half,
            (((0,), (0,)), ((), ())),
            preferred_element_type=jnp.float32,
        )
        return ((grad_proto, member_sum), row_terms)

    empty_sums = jnp.zeros((local_k, feature_dim), jnp.float32)
    (proto_fine, member_sum), row_terms = lax.scan(
        grads_block, (empty_sums, empty_sums), (row_blocks, label_blocks, total_blocks)
    )
    row_grad = lax.psum_scatter(
        row_terms.reshape(gathered_rows, feature_dim), "group", scatter_dimension=0, tiled=True
    )
    grad_embeddings = inverse * (
        row_grad - unit_rows * jnp.sum(unit_rows * row_grad, axis=1, keepdims=True)
    )
    weighting = total_k / total_rows
    logits = 10.0 * lax.dot_general(
        prototypes, coarse_protos, (((1,), (1,)), ((), ())), preferred_element_type=jnp.float32
    )
    largest = jnp.max(logits, axis=1)
    coarse_total = largest + jnp.log(jnp.sum(jnp.exp(logits - largest[:, None]), axis=1))
    member = jnp.arange(coarse_count, dtype=jnp.int32)[None, :] == coarse_labels[:, None]
    target = jnp.sum(jnp.where(member, logits, 0.0), axis=1)
    delta = (10.0 * (jnp.exp(logits - coarse_total[:, None]) - member.astype(jnp.float32))).astype(
        jnp.bfloat16
    )
    proto_part = jnp.dot(delta, coarse_protos, preferred_element_type=jnp.float32)
    coarse_part_grad = lax.dot_general(
        delta, prototypes, (((0,), (0,)), ((), ())), preferred_element_type=jnp.float32
    )
    coarse_loss = jnp.sum(coarse_total - target)
    fine_part, members = lax.psum((proto_fine, member_sum), "rows")
    coarse_summed = lax.psum(coarse_part_grad, "group")
    proto_float = prototypes.astype(jnp.float32)
    gradient = weighting * fine_part + proto_part
    proto_norm = jnp.sqrt(jnp.sum(proto_float * proto_float, axis=1, keepdims=True) + 1e-06)
    direction = members * lax.rsqrt(jnp.sum(members * members, axis=1, keepdims=True) + 1e-06)
    new_prototypes = 0.5 * proto_float + 0.5 * proto_norm * direction
    coarse_loss = coarse_loss * (row_index == 0).astype(jnp.float32)
    fine_summed, coarse_loss_summed = lax.psum((fine_loss, coarse_loss), ("rows", "group"))
    total_loss = fine_summed / total_rows + coarse_loss_summed / total_k
    grad_coarse = coarse_count / total_k * coarse_summed
    return (grad_embeddings, gradient, new_prototypes, grad_coarse, total_loss)


def solution(mesh):
    in_specs = (P(("rows", "group"), None), P(("rows", "group")), P("group", None), P(), P("group"))
    out_specs = (P(("rows", "group"), None), P("group", None), P("group", None), P(), P())
    return jax.shard_map(body, mesh=mesh, in_specs=in_specs, out_specs=out_specs, check_vma=False)
```

profile of v0, /device:TPU:1, one launch (start us, length us, event | category | flops | bytes accessed | tf_op | source)
XLA Modules:
  0.0 492.8 jit_solution(382777586622842472)
XLA Ops:
  10.1 1.8 multiply_reduce_fusion.1
  13.9 2.4 fusion.35
  16.4 19.3 %all-gather = s32[16,1,256]{2,1,0:T(1,128)S(1)} all-gather(s32[1,1,256]{2,1,0:T(1,128)S(1)} %bitcast.88), channel_id=1, replica_groups=mesh['rows'=16,'group'=16] {'group'}, dimensions={0}, use_global_device_ids=true | all-gather | bytes 17408 | tf_op jit(solution)/shard_map/all_gather | solution.py:23
  35.8 28.2 %all-gather.3.cloned.1.call-done = bf16[4096,256]{1,0:T(8,128)(2,1)} async-done(((bf16[256,256]{1,0:T(8,128)(2,1)}), bf16[4096,256]{1,0:T(8,128)(2,1)}) %all-gather.3.cloned.1.call-update) | async-done | bytes 2097168 | tf_op jit(solution)/shard_map/all_gather | solution.py:22
  64.0 21.0 %while.30 = (s32[]{:T(128)}, f32[8,512]{1,0:T(8,128)S(1)}, f32[8,512]{1,0:T(8,128)S(1)}, f32[8,512]{1,0:T(8,128)S(1)}, bf16[8,512,256]{2,1,0:T(8,128)(2,1)}, /*i...) while((s32[]{:T(128)}, f32[8,512]{1,0:T(8,128)S(1)}, ...), condition=%wide.region_5.6_spmd.clone, body=%wide.region_1.5_spmd.clone.sunk | while | flops 272628224 | bytes 5007481 | solution.py:45
  85.1 58.0 %pmax.7 = f32[4096]{0:T(1024)S(1)} all-reduce(f32[4096]{0:T(1024)S(1)} %bitcast.80), channel_id=1, replica_groups=mesh['rows'=16,'group'=16] {'group'}, use_global_device_ids=true, to_apply=%region_6.7 | all-reduce | flops 4096 | bytes 32768 | tf_op jit(solution)/shard_map/pmax | solution.py:49
  143.0 56.0 %all-reduce.1 = (f32[4096]{0:T(1024)S(1)}, f32[4096]{0:T(1024)S(1)}) all-reduce(f32[4096]{0:T(1024)S(1)} %exponential_multiply_fusion, f32[4096]{0:T(1024)S(1)} %bitcast.82), channel_id=1, replica_groups=mesh['rows'=16,'group'=16] {'group'}, use_global_device_ids=true, to_apply=%region_7.8 | all-reduce | flops 8192 | bytes 65536 | tf_op jit(solution)/shard_map/psum | solution.py:50
  199.1 56.0 %while.31 = (s32[]{:T(128)}, f32[1024,256]{1,0:T(8,128)S(1)}, f32[1024,256]{1,0:T(8,128)S(1)}, f32[8,512,256]{2,1,0:T(8,128)}, bf16[8,512,256]{2,1,0:T(8,128)(2,...) while((s32[]{:T(128)}, f32[1024,256]{1,0:T(8,128)S(1)}, ...), condition=%wide.region_9.10_spmd.clone, body=%wide.region_8.9_spmd.clone.sunk | while | flops 1078984704 | bytes 9713808 | solution.py:79
  200.9 2.2 fusion.65
  207.9 2.2 fusion.65
  214.9 2.2 fusion.65
  221.9 2.2 fusion.65
  224.0 1.8 convolution_add_fusion.3
  228.9 2.2 fusion.65
  235.9 2.2 fusion.65
  242.9 2.2 fusion.65
  249.9 2.2 fusion.65
  258.6 2.3 broadcast_multiply_fusion
  260.8 103.4 %all-reduce = (f32[]{:T(128)}, f32[]{:T(128)}) all-reduce(f32[]{:T(128)} %fusion.34, f32[]{:T(128)S(6)} %mul.132), channel_id=1, replica_groups=mesh['rows'=16,'group'=16] {'rows','group'}, use_global_device_ids=true, to_apply=%region_21.22 | all-reduce | flops 2 | bytes 16 | tf_op jit(solution)/shard_map/psum | solution.py:112
  365.5 31.8 %all-reduce.8.cloned.1.call-done = (f32[1024,256]{1,0:T(8,128)}, f32[1024,256]{1,0:T(8,128)}) async-done(((f32[1024,256]{1,0:T(8,128)}, f32[1024,256]{1,0:T(8,128)}), (f32[1024,256]{1,0:T(8,128)}, f32[1024,256]{1,0:T(8,128)})) %all-reduce.8.cloned.1.call-update) | async-done | bytes 2097168 | tf_op jit(solution)/shard_map/psum | solution.py:104
  398.8 2.5 fusion.25
  401.3 5.0 %convolution_add_fusion.1 = f32[1024,256]{1,0:T(8,128)} fusion(bf16[1024,256]{1,0:T(8,128)(2,1)S(1)} %copy-done, f32[1024,256]{1,0:T(8,128)} %get-tuple-element.187, f32[1024,1024]{0,1:T(8,128)} %copy-done.4, s32[1024]{0:T(1024)S(1)} %copy-done.6, f32[1024]{0:T(1024)S(1)} %get-tuple-element.190), kind=kOutput, calls=%fused_computation.38 | convolution fusion | flops 544735232 | bytes 6823936 | tf_op jit(solution)/shard_map/dot_general | solution.py:99
  406.3 76.0 %reduce-scatter.2.cloned.1.call-done = f32[256,256]{1,0:T(8,128)} async-done(((f32[4096,256]{1,0:T(8,128)}), f32[256,256]{1,0:T(8,128)}) %reduce-scatter.2.cloned.1.call-update) | async-done | bytes 262160 | tf_op jit(solution)/shard_map/reduce_scatter | solution.py:82
  483.4 1.8 fusion.32
  (137 shorter events, 67.8 us)
Async XLA Ops:
  7.2 2.9 copy-start
  7.2 4.8 copy-start.6
  7.2 56.8 %all-gather.3.cloned.1.call-start = ((), (), s32[]{:S(2)}) async-start(), calls=%async_computation.1 | async-start | bytes 2228224 | tf_op jit(solution)/shard_map/all_gather | solution.py:22
  10.0 3.8 copy-start.1
  10.0 248.5 %all-reduce.6.cloned.1.call-start = ((), (), s32[]{:S(2)}) async-start(), calls=%async_computation.3 | async-start | bytes 2097152 | tf_op jit(solution)/shard_map/psum | solution.py:105
  11.9 1.9 copy-start.4
  13.9 2.5 copy-start.7
  16.3 381.1 %all-reduce.8.cloned.1.call-start = ((), (), s32[]{:S(2)}) async-start(), calls=%async_computation.4 | async-start | bytes 4194304 | tf_op jit(solution)/shard_map/psum | solution.py:104
  255.1 1.0 copy-start.2
  255.1 1.3 copy-start.3
  256.4 225.8 %reduce-scatter.2.cloned.1.call-start = ((), (), s32[]{:S(2)}) async-start(), calls=%async_computation.2 | async-start | bytes 4456448 | tf_op jit(solution)/shard_map/reduce_scatter | solution.py:82
  401.3 80.9 %copy-start.5 = (bf16[256,256]{1,0:T(8,128)(2,1)S(1)}, bf16[256,256]{1,0:T(8,128)(2,1)}, u32[]{:S(2)}) copy-start(bf16[256,256]{1,0:T(8,128)(2,1)} %param.9) | copy-start | bytes 393220
Sparse Core Ops, SparseCore 0:
  11.0 52.8 all-gather.2
  67.8 95.9 all-reduce.5
  256.6 140.7 all-reduce.7
  400.8 81.3 reduce-scatter.1
where the time goes:
time: 495 us; the launch traced here: 493 us
  blocking collectives  237 us (48%)
  waiting for transfers between devices  137 us (28%)
  matrix products  76.9 us (16%)
  other arithmetic  21.9 us (4%)
  between operations  17 us (3%)
    psum x1, blocking collectives, body(): lax.psum((fine_loss, coarse_loss), ('rows', 'group'))  103 us
    reduce_scatter x1, waiting for transfers between devices, body(): lax.psum_scatter(row_terms.reshape(gathered_rows, feature_dim), 'group',...  76 us
    pmax x1, blocking collectives, body(): global_peak = lax.pmax(row_peak, 'group')  58 us
    psum x1, blocking collectives, body(): lax.psum((row_total * jnp.exp(row_peak - global_peak), row_target), 'group')  56 us
    psum x1, waiting for transfers between devices, body(): fine_part, members = lax.psum((proto_fine, member_sum), 'rows')  31.8 us
    all_gather x1, waiting for transfers between devices, body(): gathered = lax.all_gather(unit_half, 'group', axis=0, tiled=True)  28.2 us
    dot_general x16, matrix products, scores(): lax.dot_general(rows_half, prototypes, (((1,), (1,)), ((), ())), preferre...  26.2 us
    all_gather x1, blocking collectives, body(): gathered_labels = lax.all_gather(fine_labels, 'group', axis=0, tiled=True)  19.3 us
  transfers between devices with their start and end apart: 4, of which 3 were waited for; matrix products, arithmetic and copies ran while one was open for 19% of the time, Pallas kernels for 0%

commit v1 on v0

v1 whole, which is shorter than its diff:
```python
import functools

import jax
import jax.numpy as jnp
from jax import lax
from jax.experimental import pallas as pl
from jax.experimental.pallas import tpu as pltpu
from jax.sharding import PartitionSpec as P

MESH = pl.DeviceIdType.MESH
F32 = jnp.float32
BF16 = jnp.bfloat16
ROWS = 256
D = 256
KL = 1024
KC = 1024
G = 16
NCH = KL // 256
N_GATHER = 40
NT = (((1,), (1,)), ((), ()))


def dot(a, b):
    return jnp.dot(a, b, preferred_element_type=F32)


def dot_nt(a, b):
    return lax.dot_general(a, b, NT, preferred_element_type=F32)


def column_sum(value):
    return jnp.sum(value, axis=0, keepdims=True)


def total(value):
    return jnp.sum(jnp.sum(value, axis=0, keepdims=True), axis=1, keepdims=True)


def kernel(
    emb, lab, protos, coarse, clab,
    o_emb, o_pg, o_new, o_cg, o_loss,
    gbuf, labs, unit_s, inv_s, protos_t, coarse_t, lscr, ohs, ebuf, obuf, lbuf, us, rout, rin, own_rt,
    mem, soft, cg, cpart_t, cpart, stats, mmax, wbuf,
    cg_out, cg_in, cg_all, cg_fin, core_in, z_out, z_in, fin, loss_core, loss_z,
    gs, gr, labs_s, labs_r, cgo_s, cgo_r, cga_s, cga_r, cgz_s, cgz_r, st_s, st_r, rw_s, rw_r,
    co_s, co_r, zo_s, zo_r, za_s, za_r, ca_s, ca_r, ls_s, ls_r,
):
    r = lax.axis_index("rows")
    g = lax.axis_index("group")
    z, c = r // 2, lax.rem(r, 2)
    x, y = g // 4, lax.rem(g, 4)
    other = r + 1 - 2 * c

    def blk(dx, dy):
        return lax.rem(x + dx, 4) * 4 + lax.rem(y + dy, 4)

    def plane(d):
        return (r, lax.rem(g + d, G))

    def column(d):
        return (lax.rem(r + 2 * d, 16), g)

    def zof(d):
        return lax.rem(z + d, 8)

    barrier = pltpu.get_barrier_semaphore()
    for d in range(1, G):
        pl.semaphore_signal(barrier, inc=1, device_id=plane(d), device_id_type=MESH)
    for d in range(1, 8):
        pl.semaphore_signal(barrier, inc=1, device_id=column(d), device_id_type=MESH)
    pl.semaphore_signal(barrier, inc=1, device_id=(other, g), device_id_type=MESH)

    e32 = emb[...].astype(F32)
    inv = lax.rsqrt(jnp.sum(e32 * e32, axis=1, keepdims=True) + 1e-06)
    unit = e32 * inv
    unit_s[...] = unit
    inv_s[...] = jnp.broadcast_to(inv, (ROWS, 128))
    gbuf[g] = unit.astype(BF16)
    labs[g] = lab[...]

    for i in range(NCH):
        protos_t[:, i * 256 : (i + 1) * 256] = protos[i * 256 : (i + 1) * 256, :].astype(F32).T.astype(BF16)
        coarse_t[:, i * 256 : (i + 1) * 256] = coarse[i * 256 : (i + 1) * 256, :].astype(F32).T.astype(BF16)

    iota = lax.broadcasted_iota(jnp.int32, (256, 256), 0)
    cg[...] = jnp.zeros_like(cg)
    mem[...] = jnp.zeros_like(mem)

    def coarse_step(kb, closs):
        cols = pl.ds(pl.multiple_of(kb * 256, 256), 256)
        u = protos[cols, :]
        peak = jnp.full((1, 256), -jnp.inf, F32)
        for i in range(NCH):
            logits = 10.0 * dot_nt(coarse[i * 256 : (i + 1) * 256, :], u)
            lscr[i * 256 : (i + 1) * 256, :] = logits
            peak = jnp.maximum(peak, jnp.max(logits, axis=0, keepdims=True))
        expsum = jnp.zeros((1, 256), F32)
        target = jnp.zeros((1, 256), F32)
        labels = clab[pl.ds(kb, 1), :]
        for i in range(NCH):
            logits = lscr[i * 256 : (i + 1) * 256, :]
            target = target + column_sum(jnp.where(iota == labels - i * 256, logits, 0.0))
            e = jnp.exp(logits - peak)
            expsum = expsum + column_sum(e)
            lscr[i * 256 : (i + 1) * 256, :] = e
        share = 1.0 / expsum
        for i in range(NCH):
            member = (iota == labels - i * 256).astype(F32)
            ohs[i * 256 : (i + 1) * 256, :] = (10.0 * (lscr[i * 256 : (i + 1) * 256, :] * share - member)).astype(BF16)
        cpart_t[:, cols] = dot(coarse_t[...], ohs[...])
        for i in range(NCH):
            cg[i * 256 : (i + 1) * 256, :] += dot(ohs[i * 256 : (i + 1) * 256, :], u)
        return closs + total(peak + jnp.log(expsum) - target)

    coarse_loss = lax.fori_loop(0, NCH, coarse_step, jnp.zeros((1, 1), F32))

    pl.semaphore_wait(barrier, 23)

    A, B = (0, 128), (128, 128)
    A0, A1, B0, B1 = (0, 64), (64, 64), (128, 64), (192, 64)
    count = [0]

    def send(block, rows, dx, dy):
        k = count[0]
        count[0] += 1
        piece = gbuf.at[block, pl.ds(*rows)]
        cp = pltpu.make_async_remote_copy(
            piece, piece, gs.at[k], gr.at[k], device_id=(r, blk(dx, dy)), device_id_type=MESH
        )
        cp.start()
        return cp

    def both_y(block):
        return send(block, A, 0, 1), send(block, A, 0, 3)

    def both_x(block):
        return send(block, B, 1, 0), send(block, B, 3, 0)

    sends, tails = [], []

    def on_y(cp, dx, up):
        cp.wait_recv()
        out = send(blk(dx, 3 if up else 1), A0 if up else A1, 0, 1 if up else 3)
        tails.append(out)
        return out

    def on_x(cp, dy, up):
        cp.wait_recv()
        out = send(blk(3 if up else 1, dy), B0 if up else B1, 1 if up else 3, 0)
        tails.append(out)
        return out

    a1, a2 = send(g, A, 1, 0), send(g, A, 3, 0)
    b1, b2 = send(g, B, 0, 1), send(g, B, 0, 3)
    a3, a4 = both_y(g)
    b3, b4 = both_x(g)

    def lab_copy(d):
        return pltpu.make_async_remote_copy(
            labs.at[g], labs.at[g], labs_s.at[d], labs_r.at[d], device_id=plane(d), device_id_type=MESH
        )

    def lab_arrival(d):
        slot = labs.at[lax.rem(g + G - d, G)]
        return pltpu.make_async_remote_copy(
            slot, slot, labs_s.at[d], labs_r.at[d], device_id=plane(d), device_id_type=MESH
        )

    @pl.loop(1, G)
    def _(d):
        lab_copy(d).start()

    base = c * 512 + z * 64
    for q in range(G):
        cg_out[q] = cg[pl.ds(pl.multiple_of(base + 8 * (q // 2), 8), 8), (q % 2) * 128 : (q % 2) * 128 + 128]

    def cgo_copy(d):
        return pltpu.make_async_remote_copy(
            cg_out.at[lax.rem(g + d, G)], cg_in.at[d], cgo_s.at[d], cgo_r.at[d], device_id=plane(d), device_id_type=MESH
        )

    @pl.loop(1, G)
    def _(d):
        cgo_copy(d).start()

    def first_pass(i):
        u = gbuf[i]
        peak = jnp.full((1, 256), -jnp.inf, F32)
        for j in range(NCH):
            logits = dot_nt(protos[j * 256 : (j + 1) * 256, :], u)
            lscr[j * 256 : (j + 1) * 256, :] = logits
            peak = jnp.maximum(peak, jnp.max(logits, axis=0, keepdims=True))
        expsum = jnp.zeros((1, 256), F32)
        labels = labs[i] - g * KL
        for j in range(NCH):
            rows = slice(j * 256, (j + 1) * 256)
            e = jnp.exp(10.0 * (lscr[rows, :] - peak))
            expsum = expsum + column_sum(e)
            ebuf[i, rows, :] = e.astype(BF16)
            member = (iota == labels - j * 256).astype(F32).astype(BF16)
            ohs[rows, :] = member
            mem[rows, :] += dot(member, u)
        obuf[i] = dot(protos_t[...], ebuf[i])
        lbuf[i] = dot(protos_t[...], ohs[...]).astype(BF16)
        mmax[pl.ds(i, 1), :] = 10.0 * peak
        stats[g, pl.ds(i, 1), :] = 10.0 * peak + jnp.log(expsum)

    first_pass(g)

    a1.wait_recv()
    f1 = send(blk(3, 0), A0, 1, 0)
    p1, p2 = both_y(blk(3, 0))
    b1.wait_recv()
    g1 = send(blk(0, 3), B0, 0, 1)
    q1, q2 = both_x(blk(0, 3))
    a2.wait_recv()
    f2 = send(blk(1, 0), A1, 3, 0)
    p3, p4 = both_y(blk(1, 0))
    b2.wait_recv()
    g2 = send(blk(0, 1), B1, 0, 3)
    q3, q4 = both_x(blk(0, 1))
    sends += [a1, a2, b1, b2, a3, a4, b3, b4, f1, f2, g1, g2, p1, p2, p3, p4, q1, q2, q3, q4]
    a3f, b3f, a4f, b4f = on_y(a3, 0, True), on_x(b3, 0, True), on_y(a4, 0, False), on_x(b4, 0, False)

    @pl.loop(1, G)
    def _(d):
        lab_arrival(d).wait_recv()

    @pl.loop(0, 4)
    def _(k):
        far = 1 + 2 * lax.rem(k, 2)
        first_pass(blk((1 - k // 2) * far, (k // 2) * far))

    f1.wait_recv()
    f2.wait_recv()
    p5, p6 = both_y(blk(2, 0))
    g1.wait_recv()
    g2.wait_recv()
    q5, q6 = both_x(blk(0, 2))
    sends += [p5, p6, q5, q6]
    p1f, q1f, p2f, q2f = on_y(p1, 3, True), on_x(q1, 3, True), on_y(p2, 3, False), on_x(q2, 3, False)
    p3f, q3f, p4f, q4f = on_y(p3, 1, True), on_x(q3, 1, True), on_y(p4, 1, False), on_x(q4, 1, False)
    for cp in (a3f, b3f, a4f, b4f):
        cp.wait_recv()

    @pl.loop(0, 4)
    def _(k):
        first_pass(blk(1 + 2 * (k // 2), 1 + 2 * lax.rem(k, 2)))

    p5f, q5f, p6f, q6f = on_y(p5, 2, True), on_x(q5, 2, True), on_y(p6, 2, False), on_x(q6, 2, False)

    @pl.loop(1, G)
    def _(d):
        cgo_copy(d).wait_recv()

    tile = cg_out[g]
    for d in range(1, G):
        tile = tile + cg_in[d]
    cg_all[g] = (KC / (KL * G)) * tile

    def cga_copy(d):
        return pltpu.make_async_remote_copy(
            cg_all.at[g], cg_all.at[g], cga_s.at[d], cga_r.at[d], device_id=plane(d), device_id_type=MESH
        )

    def cga_arrival(d):
        slot = cg_all.at[lax.rem(g + G - d, G)]
        return pltpu.make_async_remote_copy(
            slot, slot, cga_s.at[d], cga_r.at[d], device_id=plane(d), device_id_type=MESH
        )

    @pl.loop(1, G)
    def _(d):
        cga_copy(d).start()

    for cp in (p1f, q1f, p2f, q2f, p3f, q3f, p4f, q4f):
        cp.wait_recv()

    @pl.loop(0, 6)
    def _(k):
        late = lax.min(k // 2, 1)
        m = k - 2
        even = 1 + 2 * lax.rem(k, 2)
        lines = k // 4
        dx0, dy0 = 2 - 2 * k, 2 * k
        dx1 = 2 * (1 - lines) + even * lines
        dy1 = even * (1 - lines) + 2 * lines
        first_pass(blk((1 - late) * dx0 + late * dx1, (1 - late) * dy0 + late * dy1))

    @pl.loop(1, G)
    def _(d):
        cga_arrival(d).wait_recv()

    for q in range(G):
        cg_fin[c, z, (q // 2) * 8 : (q // 2) * 8 + 8, (q % 2) * 128 : (q % 2) * 128 + 128] = cg_all[q].astype(BF16)

    def cgz_copy(d):
        slot = cg_fin.at[c, z]
        return pltpu.make_async_remote_copy(
            slot, slot, cgz_s.at[d], cgz_r.at[d], device_id=column(d), device_id_type=MESH
        )

    def cgz_arrival(d):
        slot = cg_fin.at[c, zof(8 - d)]
        return pltpu.make_async_remote_copy(
            slot, slot, cgz_s.at[d], cgz_r.at[d], device_id=column(d), device_id_type=MESH
        )

    @pl.loop(1, 8)
    def _(d):
        cgz_copy(d).start()

    for cp in (p5f, q5f, p6f, q6f):
        cp.wait_recv()
    first_pass(blk(2, 2))

    target = 10.0 * total(mem[...] * protos[...].astype(F32))
    first = lax.broadcasted_iota(jnp.int32, (8, 256), 0) == 0
    stats[g, G : G + 8, :] = jnp.where(first, target, coarse_loss)

    def st_copy(d):
        return pltpu.make_async_remote_copy(
            stats.at[g], stats.at[g], st_s.at[d], st_r.at[d], device_id=plane(d), device_id_type=MESH
        )

    def st_arrival(d):
        slot = stats.at[lax.rem(g + G - d, G)]
        return pltpu.make_async_remote_copy(
            slot, slot, st_s.at[d], st_r.at[d], device_id=plane(d), device_id_type=MESH
        )

    @pl.loop(1, G)
    def _(d):
        st_copy(d).start()

    def core_copy(t):
        return pltpu.make_async_remote_copy(
            z_out.at[t, 1 - c], core_in.at[t], co_s.at[t], co_r.at[t], device_id=(other, g), device_id_type=MESH
        )

    def z_copy(t, d):
        return pltpu.make_async_remote_copy(
            z_out.at[t, c, zof(d)], z_in.at[t, d], zo_s.at[t, d], zo_r.at[t, d],
            device_id=column(d), device_id_type=MESH,
        )

    def za_copy(t, d):
        slot = fin.at[t, c, z]
        return pltpu.make_async_remote_copy(
            slot, slot, za_s.at[t, d], za_r.at[t, d], device_id=column(d), device_id_type=MESH
        )

    def za_arrival(t, d):
        slot = fin.at[t, c, zof(8 - d)]
        return pltpu.make_async_remote_copy(
            slot, slot, za_s.at[t, d], za_r.at[t, d], device_id=column(d), device_id_type=MESH
        )

    def ca_copy(t):
        slot = fin.at[t, c]
        return pltpu.make_async_remote_copy(
            slot, slot, ca_s.at[t], ca_r.at[t], device_id=(other, g), device_id_type=MESH
        )

    def ca_arrival(t):
        slot = fin.at[t, 1 - c]
        return pltpu.make_async_remote_copy(
            slot, slot, ca_s.at[t], ca_r.at[t], device_id=(other, g), device_id_type=MESH
        )

    def core_send(t, src):
        half = src[pl.ds(pl.multiple_of((1 - c) * 512, 512), 512), :].astype(BF16)
        z_out[t, 1 - c] = half.reshape(8, 64, D)
        core_copy(t).start()

    def core_merge(t, src):
        core_copy(t).wait_recv()
        half = src[pl.ds(pl.multiple_of(c * 512, 512), 512), :].reshape(8, 64, D)
        z_out[t, c] = (half + core_in[t].astype(F32)).astype(BF16)

        @pl.loop(1, 8)
        def _(d):
            z_copy(t, d).start()

    def z_merge(t):
        @pl.loop(1, 8)
        def _(d):
            z_copy(t, d).wait_recv()

        acc = z_out[t, c, z].astype(F32)
        for d in range(1, 8):
            acc = acc + z_in[t, d].astype(F32)
        fin[t, c, z] = acc.astype(BF16)

        @pl.loop(1, 8)
        def _(d):
            za_copy(t, d).start()

    def z_gathered(t):
        @pl.loop(1, 8)
        def _(d):
            za_arrival(t, d).wait_recv()

        ca_copy(t).start()

    core_send(0, mem)
    for j in range(NCH):
        rows = slice(j * 256, (j + 1) * 256)
        cpart[rows, :] = cpart_t[:, rows].T
    core_merge(0, mem)

    @pl.loop(1, G)
    def _(d):
        st_arrival(d).wait_recv()

    lse_peak = stats[0, 0:G, :]
    for j in range(1, G):
        lse_peak = jnp.maximum(lse_peak, stats[j, 0:G, :])
    lse_sum = jnp.zeros((G, 256), F32)
    extra = jnp.zeros((8, 256), F32)
    for j in range(G):
        lse_sum = lse_sum + jnp.exp(stats[j, 0:G, :] - lse_peak)
        extra = extra + stats[j, G : G + 8, :]
    log_total = lse_peak + jnp.log(lse_sum)
    wbuf[...] = jnp.exp(mmax[...] - log_total)
    loss_own = total(log_total) - extra[0:1, 0:1]
    coarse_all = extra[1:2, 0:1]

    def rw_copy(d):
        return pltpu.make_async_remote_copy(
            rout.at[d], rin.at[d], rw_s.at[d], rw_r.at[d], device_id=plane(d), device_id_type=MESH
        )

    def row_terms(i):
        return 10.0 * (obuf[i] * wbuf[pl.ds(i, 1), :] - lbuf[i].astype(F32))

    @pl.loop(1, G)
    def _(d):
        rout[d] = row_terms(lax.rem(g + d, G)).astype(BF16)
        rw_copy(d).start()

    own_rt[...] = row_terms(g)

    @pl.loop(0, G)
    def _(i):
        w_col = jnp.broadcast_to(wbuf[pl.ds(i, 1), :], (128, 256)).T
        for j in range(2):
            us[i, :, j * 128 : (j + 1) * 128] = (gbuf[i, :, j * 128 : (j + 1) * 128].astype(F32) * w_col).astype(BF16)

    for j in range(NCH):
        rows = slice(j * 256, (j + 1) * 256)
        soft[rows, :] = jnp.zeros((256, D), F32)

        @pl.loop(0, G)
        def _(i):
            soft[rows, :] += dot(ebuf[i, rows, :], us[i])

    core_send(1, soft)
    loss_core[0] = jnp.broadcast_to(loss_own, (8, 128))
    lcp = pltpu.make_async_remote_copy(
        loss_core.at[0], loss_core.at[1], ls_s.at[0], ls_r.at[0], device_id=(other, g), device_id_type=MESH
    )
    lcp.start()
    core_merge(1, soft)
    lcp.wait_recv()
    loss_z[0] = loss_core[0] + loss_core[1]

    def lz_copy(d):
        return pltpu.make_async_remote_copy(
            loss_z.at[0], loss_z.at[d], ls_s.at[d], ls_r.at[d], device_id=column(d), device_id_type=MESH
        )

    @pl.loop(1, 8)
    def _(d):
        lz_copy(d).start()

    @pl.loop(1, 8)
    def _(d):
        cgz_arrival(d).wait_recv()

    cg_mine, cg_theirs = cg_fin.at[c], cg_fin.at[1 - c]
    cgc = pltpu.make_async_remote_copy(
        cg_mine, cg_mine, cgz_s.at[0], cgz_r.at[0], device_id=(other, g), device_id_type=MESH
    )
    cgc_in = pltpu.make_async_remote_copy(
        cg_theirs, cg_theirs, cgz_s.at[0], cgz_r.at[0], device_id=(other, g), device_id_type=MESH
    )
    cgc.start()
    z_merge(0)
    cgc_in.wait_recv()
    o_cg[...] = cg_fin[...].reshape(KC, D).astype(F32)
    z_merge(1)
    z_gathered(0)
    ca_arrival(0).wait_recv()
    for j in range(NCH):
        rows = slice(j * 256, (j + 1) * 256)
        members = fin[0, j // 2, (j % 2) * 4 : (j % 2) * 4 + 4].reshape(256, D).astype(F32)
        p32 = protos[rows, :].astype(F32)
        norm = jnp.sqrt(jnp.sum(p32 * p32, axis=1, keepdims=True) + 1e-06)
        length = lax.rsqrt(jnp.sum(members * members, axis=1, keepdims=True) + 1e-06)
        o_new[rows, :] = 0.5 * p32 + (0.5 * norm) * (members * length)
        cpart[rows, :] = cpart[rows, :] - 2.5 * members

    acc = own_rt[...]
    for d in range(1, G):
        rw_copy(d).wait_recv()
        acc = acc + rin[d].astype(F32)
    own_rt[...] = acc
    row_grad = own_rt[...].T
    unit = unit_s[...]
    inv = inv_s[:, 0:1]
    o_emb[...] = inv * (row_grad - unit * jnp.sum(unit * row_grad, axis=1, keepdims=True))

    @pl.loop(1, 8)
    def _(d):
        lz_copy(d).wait_recv()

    fine = loss_z[0]
    for d in range(1, 8):
        fine = fine + loss_z[d]
    o_loss[...] = fine[0:1, 0:1] * (1.0 / (G * G * ROWS)) + coarse_all * (1.0 / (KL * G))

    z_gathered(1)
    ca_arrival(1).wait_recv()
    for j in range(NCH):
        rows = slice(j * 256, (j + 1) * 256)
        part = fin[1, j // 2, (j % 2) * 4 : (j % 2) * 4 + 4].reshape(256, D).astype(F32)
        o_pg[rows, :] = cpart[rows, :] + 2.5 * part

    for cp in sends + tails:
        cp.wait_send()

    @pl.loop(1, G)
    def _(d):
        lab_copy(d).wait_send()
        cgo_copy(d).wait_send()
        cga_copy(d).wait_send()
        st_copy(d).wait_send()
        rw_copy(d).wait_send()

    @pl.loop(1, 8)
    def _(d):
        cgz_copy(d).wait_send()
        lz_copy(d).wait_send()
        for t in range(2):
            z_copy(t, d).wait_send()
            za_copy(t, d).wait_send()

    cgc.wait_send()
    lcp.wait_send()
    for t in range(2):
        core_copy(t).wait_send()
        ca_copy(t).wait_send()


def body(embeddings, fine_labels, prototypes, coarse_protos, coarse_labels):
    vmem = pl.BlockSpec(memory_space=pltpu.VMEM)
    sem = pltpu.SemaphoreType.DMA
    scratch = [
        pltpu.VMEM((G, ROWS, D), BF16),
        pltpu.VMEM((G, 1, ROWS), jnp.int32),
        pltpu.VMEM((ROWS, D), F32),
        pltpu.VMEM((ROWS, 128), F32),
        pltpu.VMEM((D, KL), BF16),
        pltpu.VMEM((D, KC), BF16),
        pltpu.VMEM((KL, ROWS), F32),
        pltpu.VMEM((KL, ROWS), BF16),
        pltpu.VMEM((G, KL, ROWS), BF16),
        pltpu.VMEM((G, D, ROWS), F32),
        pltpu.VMEM((G, D, ROWS), BF16),
        pltpu.VMEM((G, ROWS, D), BF16),
        pltpu.VMEM((G, D, ROWS), BF16),
        pltpu.VMEM((G, D, ROWS), BF16),
        pltpu.VMEM((D, ROWS), F32),
        pltpu.VMEM((KL, D), F32),
        pltpu.VMEM((KL, D), F32),
        pltpu.VMEM((KC, D), F32),
        pltpu.VMEM((D, KL), F32),
        pltpu.VMEM((KL, D), F32),
        pltpu.VMEM((G, G + 8, ROWS), F32),
        pltpu.VMEM((G, ROWS), F32),
        pltpu.VMEM((G, ROWS), F32),
        pltpu.VMEM((G, 8, 128), F32),
        pltpu.VMEM((G, 8, 128), F32),
        pltpu.VMEM((G, 8, 128), F32),
        pltpu.VMEM((2, 8, 64, D), BF16),
        pltpu.VMEM((2, 8, 64, D), BF16),
        pltpu.VMEM((2, 2, 8, 64, D), BF16),
        pltpu.VMEM((2, 8, 64, D), BF16),
        pltpu.VMEM((2, 2, 8, 64, D), BF16),
        pltpu.VMEM((2, 8, 128), F32),
        pltpu.VMEM((8, 8, 128), F32),
        sem((N_GATHER,)), sem((N_GATHER,)),
        sem((G,)), sem((G,)), sem((G,)), sem((G,)), sem((G,)), sem((G,)),
        sem((8,)), sem((8,)),
        sem((G,)), sem((G,)), sem((G,)), sem((G,)),
        sem((2,)), sem((2,)),
        sem((2, 8)), sem((2, 8)), sem((2, 8)), sem((2, 8)),
        sem((2,)), sem((2,)),
        sem((8,)), sem((8,)),
    ]
    outs = [
        jax.ShapeDtypeStruct((ROWS, D), F32),
        jax.ShapeDtypeStruct((KL, D), F32),
        jax.ShapeDtypeStruct((KL, D), F32),
        jax.ShapeDtypeStruct((KC, D), F32),
        jax.ShapeDtypeStruct((1, 1), F32),
    ]
    ge, gp, new, gc, loss = pl.pallas_call(
        kernel,
        out_shape=outs,
        in_specs=[vmem] * 5,
        out_specs=[vmem] * 5,
        scratch_shapes=scratch,
        compiler_params=pltpu.CompilerParams(
            collective_id=0, has_side_effects=True, vmem_limit_bytes=56 * 1024 * 1024
        ),
    )(embeddings, fine_labels.reshape(1, ROWS), prototypes, coarse_protos, coarse_labels.reshape(NCH, 256))
    return ge, gp, new, gc, loss.reshape(())


def solution(mesh):
    in_specs = (P(("rows", "group"), None), P(("rows", "group")), P("group", None), P(), P("group"))
    out_specs = (P(("rows", "group"), None), P("group", None), P("group", None), P(), P())
    return jax.shard_map(body, mesh=mesh, in_specs=in_specs, out_specs=out_specs, check_vma=False)
```

time: 495 us -> 102 us (0.21)
  the two profiles are of different devices: /device:TPU:1 before, /device:TPU:31 now
where the time goes in v1:
time: 102 us
  Pallas kernels  91.7 us (90%)
  local copies, waits for them, and re-layouts  7.88 us (8%)
  between operations  2.41 us (2%)
    pallas_call x1, Pallas kernels, body(): pl.pallas_call(kernel, out_shape=outs, in_specs=[vmem] * 5, out_specs=[vm...  91.7 us
    unnamed x8, local copies, waits for them, and re-layouts  6.6 us

profile of v1, /device:TPU:31, one launch (start us, length us, event | category | flops | bytes accessed | tf_op | source)
XLA Modules:
  0.0 102.0 jit_solution(7115098512502931501)
XLA Ops:
  0.6 1.3 %reshape.20.clab = s32[4,256]{1,0:T(4,128)} reshape(s32[1024]{0:T(1024)} %param.9) | data formatting | bytes 8192 | tf_op jit(solution)/shard_map/reshape | solution.py:618
  1.9 91.7 %shard_map.92 = (f32[256,256]{1,0:T(8,128)}, f32[1024,256]{1,0:T(8,128)}, f32[1024,256]{1,0:T(8,128)}, f32[1024,256]{1,0:T(8,128)}, f32[1,1]{1,0:T(1,128)}) custom-call(bf16[256,256]{1,0:T(8,128)(2,1)} %emb.1, s32[1,256]{1,0:T(1,128)} %bitcast.2, bf16[1024,256]{1,0:T(8,128)(2,1)} %protos.1, bf16[1024,256]{1,0:T(8,128)(2,1)} %coarse.1, s32[4,256]{1,0:T(4,128)} %reshape.20.clab), custom_call_target="tpu_custom_call" | custom-call | tf_op jit(solution)/shard_map/pallas_call | solution.py:609
  93.6 1.7 %copy.15 = f32[256,256]{1,0:T(8,128)} copy(f32[256,256]{1,0:T(8,128)} %get-tuple-element.20) | data formatting | bytes 524288
  95.3 0.0 copy-start.1
  95.3 2.4 %copy.16 = f32[1024,256]{1,0:T(8,128)} copy(f32[1024,256]{1,0:T(8,128)} %get-tuple-element.21) | data formatting | bytes 2097152
  97.6 0.0 copy-done.1
  97.6 0.0 copy-start
  97.6 1.0 copy.17
  98.6 0.6 copy-done
  99.3 1.0 copy.18
Async XLA Ops:
  95.3 2.4 %copy-start.1 = (f32[1024,256]{1,0:T(8,128)S(1)}, f32[1024,256]{1,0:T(8,128)}, u32[]{:S(2)}) copy-start(f32[1024,256]{1,0:T(8,128)} %get-tuple-element.22) | copy-start | bytes 3145732
  97.6 1.6 %copy-start = (f32[1024,256]{1,0:T(8,128)S(1)}, f32[1024,256]{1,0:T(8,128)}, u32[]{:S(2)}) copy-start(f32[1024,256]{1,0:T(8,128)} %get-tuple-element.23) | copy-start | bytes 3145732

commit v2 on v1

v2 whole, which is shorter than its diff:
```python
import functools

import jax
import jax.numpy as jnp
from jax import lax
from jax.experimental import pallas as pl
from jax.experimental.pallas import tpu as pltpu
from jax.sharding import PartitionSpec as P

MESH = pl.DeviceIdType.MESH
F32 = jnp.float32
BF16 = jnp.bfloat16
ROWS = 256
D = 256
KL = 1024
KC = 1024
G = 16
NCH = KL // 256
N_GATHER = 40
NT = (((1,), (1,)), ((), ()))
LOG2E = 1.4426950408889634


def dot(a, b):
    return jnp.dot(a, b, preferred_element_type=F32)


def dot_nt(a, b):
    return lax.dot_general(a, b, NT, preferred_element_type=F32)


def column_sum(value):
    return jnp.sum(value, axis=0, keepdims=True)


def total(value):
    return jnp.sum(jnp.sum(value, axis=0, keepdims=True), axis=1, keepdims=True)


def rel(dx, dy):
    return (dx % 4) * 4 + dy % 4


ORDER = [(0, 0), (1, 0), (3, 0), (0, 1), (0, 3), (1, 1), (1, 3), (3, 1), (3, 3), (0, 2), (1, 2), (3, 2)]
ORDER += [(2, 0), (2, 1), (2, 3), (2, 2)]
PEERS = ORDER[1:]
SLOT = {0: 0, 1: 1, 3: 2}


def kernel(
    emb, lab, protos, coarse, clab,
    o_emb, o_pg, o_new, o_cg, o_loss,
    gbuf, labs, unit_s, inv_s, protos_t, coarse_t, lscr, lscr2, ebuf, obuf, lbuf, us, rout, rin, own_rt,
    mem, soft, cg, cpart_t, cpart, stats_a, stats_b, mmax, lt_a, wbuf,
    cg_out, cg_in, cg_all, cg_fin, core_in, z_out, z_in, fin, extra, loss_core, loss_z,
    gs, gr, labs_s, labs_r, cgo_s, cgo_r, cga_s, cga_r, cgz_s, cgz_r, sa_s, sa_r, sb_s, sb_r, ex_s, ex_r,
    rw_s, rw_r, co_s, co_r, zo_s, zo_r, za_s, za_r, ca_s, ca_r, ls_s, ls_r,
):
    r = lax.axis_index("rows")
    g = lax.axis_index("group")
    z, c = r // 2, lax.rem(r, 2)
    x, y = g // 4, lax.rem(g, 4)
    other = r + 1 - 2 * c
    xs = [lax.rem(x + i, 4) * 4 for i in range(4)]
    ys = [lax.rem(y + i, 4) for i in range(4)]

    def plane(dx, dy):
        return (r, xs[dx % 4] + ys[dy % 4])

    def column(d):
        return (lax.rem(r + 2 * d, 16), g)

    def zof(d):
        return lax.rem(z + d, 8)

    barrier = pltpu.get_barrier_semaphore()
    for d in range(1, 8):
        pl.semaphore_signal(barrier, inc=1, device_id=column(d), device_id_type=MESH)
    for p in PEERS:
        pl.semaphore_signal(barrier, inc=1, device_id=plane(*p), device_id_type=MESH)
    pl.semaphore_signal(barrier, inc=1, device_id=(other, g), device_id_type=MESH)

    e32 = emb[...].astype(F32)
    inv = lax.rsqrt(jnp.sum(e32 * e32, axis=1, keepdims=True) + 1e-06)
    unit = e32 * inv
    unit_s[...] = unit
    inv_s[...] = jnp.broadcast_to(inv, (ROWS, 128))
    gbuf[0] = unit.astype(BF16)
    labs[0] = lab[...]

    pl.semaphore_wait(barrier, 23)

    A, B = (0, 128), (128, 128)
    A0, A1, B0, B1 = (0, 64), (64, 64), (128, 64), (192, 64)
    gathers = []

    def send(bx, by, rows, dx, dy):
        k = len(gathers)
        cp = pltpu.make_async_remote_copy(
            gbuf.at[rel(bx, by), pl.ds(*rows)], gbuf.at[rel(bx - dx, by - dy), pl.ds(*rows)],
            gs.at[k], gr.at[k], device_id=plane(dx, dy), device_id_type=MESH,
        )
        cp.start()
        gathers.append(cp)
        return cp

    def both_y(bx, by):
        return send(bx, by, A, 0, 1), send(bx, by, A, 0, 3)

    def both_x(bx, by):
        return send(bx, by, B, 1, 0), send(bx, by, B, 3, 0)

    def on_y(cp, bx, up):
        cp.wait_recv()
        return send(bx, 3, A0, 0, 1) if up else send(bx, 1, A1, 0, 3)

    def on_x(cp, by, up):
        cp.wait_recv()
        return send(3, by, B0, 1, 0) if up else send(1, by, B1, 3, 0)

    def arrived(*copies):
        for cp in copies:
            cp.wait_recv()

    def exchange(src, dst, send_sem, recv_sem):
        copies = []
        for k, p in enumerate(PEERS):
            cp = pltpu.make_async_remote_copy(
                src(k), dst(rel(-p[0], -p[1])), send_sem.at[k], recv_sem.at[k],
                device_id=plane(*p), device_id_type=MESH,
            )
            cp.start()
            copies.append(cp)
        return copies

    a1, a2 = send(0, 0, A, 1, 0), send(0, 0, A, 3, 0)
    b1, b2 = send(0, 0, B, 0, 1), send(0, 0, B, 0, 3)
    a3, a4 = both_y(0, 0)
    b3, b4 = both_x(0, 0)
    lab_x = exchange(lambda k: labs.at[0], lambda s: labs.at[s], labs_s, labs_r)

    iota = lax.broadcasted_iota(jnp.int32, (256, 256), 0)
    iota_half = iota.astype(F32).astype(BF16)
    parts = [slice(j * 256, (j + 1) * 256) for j in range(NCH)]

    for rows in parts:
        protos_t[:, rows] = protos[rows, :].astype(F32).T.astype(BF16)
        coarse_t[:, rows] = coarse[rows, :].astype(F32).T.astype(BF16)

    def logits_peak(left, u):
        peak = None
        for rows in parts:
            logits = dot_nt(left[rows, :], u)
            lscr[rows, :] = logits
            peak = logits if peak is None else jnp.maximum(peak, logits)
        return jnp.max(peak, axis=0, keepdims=True)

    def add(a, b):
        return b if a is None else a + b

    def onehot(labels, j):
        near = labels - j * 256
        near = jnp.where((near >= 0) & (near < 256), near, -1).astype(F32).astype(BF16)
        return jnp.where(iota_half == near, jnp.ones((), BF16), jnp.zeros((), BF16))

    def coarse_block(kb):
        u = protos[parts[kb], :]
        labels = clab[:, parts[kb]]
        peak = logits_peak(coarse, u)
        expsum = target = out = None
        for j, rows in enumerate(parts):
            logits = lscr[rows, :]
            target = add(target, jnp.where(iota == labels - j * 256, logits, 0.0))
            e = jnp.exp2((logits - peak) * (10.0 * LOG2E))
            expsum = add(expsum, e)
            lscr2[rows, :] = e
        expsum = column_sum(expsum)
        share = 10.0 / expsum
        for j, rows in enumerate(parts):
            delta = (lscr2[rows, :] * share - jnp.where(iota == labels - j * 256, 10.0, 0.0)).astype(BF16)
            out = add(out, dot(coarse_t[:, rows], delta))
            if kb == 0:
                cg[rows, :] = dot(delta, u)
            else:
                cg[rows, :] += dot(delta, u)
        cpart_t[:, parts[kb]] = out
        return total(10.0 * (peak - column_sum(target)) + jnp.log(expsum))

    def local_labels(p):
        return labs[rel(*p)] - g * KL

    def first_pass(k, prev):
        dx, dy = ORDER[k]
        u = gbuf[rel(dx, dy)]
        peak = logits_peak(protos, u)
        labels = local_labels(ORDER[k])
        expsum = out = None
        for j, rows in enumerate(parts):
            e = jnp.exp2((lscr[rows, :] - peak) * (10.0 * LOG2E))
            expsum = add(expsum, e)
            ebuf[k, rows, :] = e.astype(BF16)
            if prev is not None:
                out = add(out, dot(protos_t[:, rows], ebuf[prev, rows, :]))
            member = dot(onehot(labels, j), u)
            if k == 0:
                mem[rows, :] = member
            else:
                mem[rows, :] += member
        if prev is not None:
            obuf[prev] = out
        mmax[k : k + 1, :] = 10.0 * peak
        lse = 10.0 * peak + jnp.log(column_sum(expsum))
        if dx == 2:
            stats_b[0, pl.ds(ys[dy], 1), :] = lse
        else:
            stats_a[0, pl.ds(SLOT[dx] * 4 + ys[dy], 1), :] = lse

    coarse_loss = coarse_block(0)
    first_pass(0, None)

    a1.wait_recv()
    f1 = send(3, 0, A0, 1, 0)
    p1, p2 = both_y(3, 0)
    b1.wait_recv()
    g1 = send(0, 3, B0, 0, 1)
    q1, q2 = both_x(0, 3)
    a2.wait_recv()
    f2 = send(1, 0, A1, 3, 0)
    p3, p4 = both_y(1, 0)
    b2.wait_recv()
    g2 = send(0, 1, B1, 0, 3)
    q3, q4 = both_x(0, 1)
    coarse_loss = coarse_loss + coarse_block(1)
    a3f, b3f, a4f, b4f = on_y(a3, 0, True), on_x(b3, 0, True), on_y(a4, 0, False), on_x(b4, 0, False)
    coarse_loss = coarse_loss + coarse_block(2)
    coarse_loss = coarse_loss + coarse_block(3)

    base = c * 512 + z * 64

    def tile_of(q):
        return cg[pl.ds(pl.multiple_of(base + 8 * (q // 2), 8), 8), (q % 2) * 128 : (q % 2) * 128 + 128]

    for q in range(G):
        cg_out[q] = tile_of(q)
    cgo_x = []
    for k, p in enumerate(PEERS):
        cp = pltpu.make_async_remote_copy(
            cg_out.at[xs[p[0]] + ys[p[1]]], cg_in.at[k], cgo_s.at[k], cgo_r.at[k],
            device_id=plane(*p), device_id_type=MESH,
        )
        cp.start()
        cgo_x.append(cp)

    arrived(*lab_x)
    arrived(f1, f2)
    p5, p6 = both_y(2, 0)
    arrived(g1, g2)
    q5, q6 = both_x(0, 2)
    first_pass(1, 0)
    first_pass(2, 1)
    p1f, q1f, p2f, q2f = on_y(p1, 3, True), on_x(q1, 3, True), on_y(p2, 3, False), on_x(q2, 3, False)
    first_pass(3, 2)
    p3f, q3f, p4f, q4f = on_y(p3, 1, True), on_x(q3, 1, True), on_y(p4, 1, False), on_x(q4, 1, False)
    first_pass(4, 3)
    first_pass(5, 4)
    p5f, q5f, p6f, q6f = on_y(p5, 2, True), on_x(q5, 2, True), on_y(p6, 2, False), on_x(q6, 2, False)
    first_pass(6, 5)
    first_pass(7, 6)
    first_pass(8, 7)

    arrived(*cgo_x)
    tile = cg_out[g]
    for k in range(G - 1):
        tile = tile + cg_in[k]
    cg_all[g] = (KC / (KL * G)) * tile
    cga_x = []
    for k, p in enumerate(PEERS):
        cp = pltpu.make_async_remote_copy(
            cg_all.at[g], cg_all.at[g], cga_s.at[k], cga_r.at[k], device_id=plane(*p), device_id_type=MESH
        )
        cp.start()
        cga_x.append(cp)

    arrived(a3f, b3f, a4f, b4f)
    first_pass(9, 8)
    arrived(p1f, p2f, p3f, p4f)
    first_pass(10, 9)
    first_pass(11, 10)
    sa_x = exchange(lambda k: stats_a.at[0], lambda s: stats_a.at[s], sa_s, sa_r)
    first_pass(12, 11)
    arrived(q1f, q2f, q3f, q4f)
    first_pass(13, 12)
    first_pass(14, 13)

    arrived(*cga_x)
    for q in range(G):
        cg_fin[c, z, (q // 2) * 8 : (q // 2) * 8 + 8, (q % 2) * 128 : (q % 2) * 128 + 128] = cg_all[q].astype(BF16)

    @functools.cache
    def cgz_copy(d):
        slot = cg_fin.at[c, z]
        return pltpu.make_async_remote_copy(
            slot, slot, cgz_s.at[d], cgz_r.at[d], device_id=column(d), device_id_type=MESH
        )

    for d in range(1, 8):
        cgz_copy(d).start()

    arrived(p5f, q5f, p6f, q6f)
    first_pass(15, 14)
    sb_x = exchange(lambda k: stats_b.at[0], lambda s: stats_b.at[s], sb_s, sb_r)

    @functools.cache
    def core_copy(t):
        return pltpu.make_async_remote_copy(
            z_out.at[t, 1 - c], core_in.at[t], co_s.at[t], co_r.at[t], device_id=(other, g), device_id_type=MESH
        )

    @functools.cache
    def z_copy(t, d):
        return pltpu.make_async_remote_copy(
            z_out.at[t, c, zof(d)], z_in.at[t, d], zo_s.at[t, d], zo_r.at[t, d],
            device_id=column(d), device_id_type=MESH,
        )

    @functools.cache
    def za_copy(t, d):
        slot = fin.at[t, c, z]
        return pltpu.make_async_remote_copy(
            slot, slot, za_s.at[t, d], za_r.at[t, d], device_id=column(d), device_id_type=MESH
        )

    @functools.cache
    def ca_copy(t):
        slot = fin.at[t, c]
        return pltpu.make_async_remote_copy(
            slot, slot, ca_s.at[t], ca_r.at[t], device_id=(other, g), device_id_type=MESH
        )

    def core_send(t, src):
        half = src[pl.ds(pl.multiple_of((1 - c) * 512, 512), 512), :].astype(BF16)
        z_out[t, 1 - c] = half.reshape(8, 64, D)
        core_copy(t).start()

    def core_merge(t, src):
        core_copy(t).wait_recv()
        half = src[pl.ds(pl.multiple_of(c * 512, 512), 512), :].reshape(8, 64, D)
        z_out[t, c] = (half + core_in[t].astype(F32)).astype(BF16)

        for d in range(1, 8):
            z_copy(t, d).start()

    def z_merge(t):
        for d in range(1, 8):
            z_copy(t, d).wait_recv()

        acc = z_out[t, c, z].astype(F32)
        for d in range(1, 8):
            acc = acc + z_in[t, d].astype(F32)
        fin[t, c, z] = acc.astype(BF16)

        for d in range(1, 8):
            za_copy(t, d).start()

    def z_gathered(t):
        for d in range(1, 8):
            za_copy(t, d).wait_recv()

        ca_copy(t).start()

    core_send(0, mem)
    target = 10.0 * total(mem[...] * protos[...].astype(F32))
    first = lax.broadcasted_iota(jnp.int32, (8, 128), 0) == 0
    extra[0] = jnp.where(first, target, coarse_loss)
    ex_x = exchange(lambda k: extra.at[0], lambda s: extra.at[s], ex_s, ex_r)
    core_merge(0, mem)

    last = None
    for rows in parts:
        last = add(last, dot(protos_t[:, rows], ebuf[15, rows, :]))
    obuf[15] = last
    for k, p in enumerate(ORDER):
        labels = local_labels(p)
        out = None
        for j, rows in enumerate(parts):
            out = add(out, dot(protos_t[:, rows], onehot(labels, j)))
        lbuf[k] = out.astype(BF16)
    for rows in parts:
        cpart[rows, :] = cpart_t[:, rows].T

    arrived(*sa_x)
    arrived(*sb_x)

    def line(a, b, dx):
        away = (dx - a) % 4
        if away == 2:
            return stats_b[rel(a, b)]
        return stats_a[rel(a, b), SLOT[away] * 4 : SLOT[away] * 4 + 4, :]

    loss_rows = None
    for dx in range(4):
        lines = [line(a, b, dx) for a in range(4) for b in range(4)]
        peak = functools.reduce(jnp.maximum, lines)
        log_total = peak + jnp.log(functools.reduce(add, [jnp.exp(v - peak) for v in lines]))
        lt_a[dx] = log_total
        loss_rows = add(loss_rows, log_total)
    for k, (dx, dy) in enumerate(ORDER):
        wbuf[k : k + 1, :] = jnp.exp(mmax[k : k + 1, :] - lt_a[dx, pl.ds(ys[dy], 1), :])

    def row_terms(k):
        return 10.0 * (obuf[k] * wbuf[k : k + 1, :] - lbuf[k].astype(F32))

    rw_x = []
    for k in range(G - 1, 0, -1):
        p = ORDER[k]
        rout[k] = row_terms(k).astype(BF16)
        cp = pltpu.make_async_remote_copy(
            rout.at[k], rin.at[k], rw_s.at[k], rw_r.at[k], device_id=plane(*p), device_id_type=MESH
        )
        cp.start()
        rw_x.append(cp)
    own_rt[...] = row_terms(0)

    for j, rows in enumerate(parts):
        acc = None
        for k, p in enumerate(ORDER):
            if j == 0:
                w_col = jnp.broadcast_to(wbuf[k : k + 1, :], (128, 256)).T
                for h in (slice(0, 128), slice(128, 256)):
                    us[k, :, h] = (gbuf[rel(*p), :, h].astype(F32) * w_col).astype(BF16)
            acc = add(acc, dot(ebuf[k, rows, :], us[k]))
        soft[rows, :] = acc

    core_send(1, soft)
    arrived(*ex_x)
    sums = functools.reduce(add, [extra[k] for k in range(G)])
    coarse_all = sums[1:2, 0:1]
    loss_core[0] = jnp.broadcast_to(total(loss_rows) - sums[0:1, 0:1], (8, 128))
    lcp = pltpu.make_async_remote_copy(
        loss_core.at[0], loss_core.at[1], ls_s.at[0], ls_r.at[0], device_id=(other, g), device_id_type=MESH
    )
    lcp.start()
    core_merge(1, soft)
    lcp.wait_recv()
    loss_z[0] = loss_core[0] + loss_core[1]

    @functools.cache
    def lz_copy(d):
        return pltpu.make_async_remote_copy(
            loss_z.at[0], loss_z.at[d], ls_s.at[d], ls_r.at[d], device_id=column(d), device_id_type=MESH
        )

    for d in range(1, 8):
        lz_copy(d).start()

    for d in range(1, 8):
        cgz_copy(d).wait_recv()

    cg_mine = cg_fin.at[c]
    cgc = pltpu.make_async_remote_copy(
        cg_mine, cg_mine, cgz_s.at[0], cgz_r.at[0], device_id=(other, g), device_id_type=MESH
    )
    cgc.start()
    z_merge(0)
    cgc.wait_recv()
    o_cg[...] = cg_fin[...].reshape(KC, D).astype(F32)
    z_merge(1)
    z_gathered(0)
    ca_copy(0).wait_recv()
    for j, rows in enumerate(parts):
        members = fin[0, j // 2, (j % 2) * 4 : (j % 2) * 4 + 4].reshape(256, D).astype(F32)
        p32 = protos[rows, :].astype(F32)
        norm = jnp.sqrt(jnp.sum(p32 * p32, axis=1, keepdims=True) + 1e-06)
        length = lax.rsqrt(jnp.sum(members * members, axis=1, keepdims=True) + 1e-06)
        o_new[rows, :] = 0.5 * p32 + (0.5 * norm) * (members * length)
        cpart[rows, :] = cpart[rows, :] - 2.5 * members

    arrived(*rw_x)
    acc = own_rt[...]
    for k in range(1, G):
        acc = acc + rin[k].astype(F32)
    row_grad = acc.T
    unit = unit_s[...]
    inv = inv_s[:, 0:1]
    o_emb[...] = inv * (row_grad - unit * jnp.sum(unit * row_grad, axis=1, keepdims=True))

    for d in range(1, 8):
        lz_copy(d).wait_recv()

    fine = functools.reduce(add, [loss_z[d] for d in range(8)])
    o_loss[...] = fine[0:1, 0:1] * (1.0 / (G * G * ROWS)) + coarse_all * (1.0 / (KL * G))

    z_gathered(1)
    ca_copy(1).wait_recv()
    for j, rows in enumerate(parts):
        part = fin[1, j // 2, (j % 2) * 4 : (j % 2) * 4 + 4].reshape(256, D).astype(F32)
        o_pg[rows, :] = cpart[rows, :] + 2.5 * part

    for cp in gathers + lab_x + cgo_x + cga_x + sa_x + sb_x + ex_x + rw_x:
        cp.wait_send()

    for d in range(1, 8):
        cgz_copy(d).wait_send()
        lz_copy(d).wait_send()
        for t in range(2):
            z_copy(t, d).wait_send()
            za_copy(t, d).wait_send()

    cgc.wait_send()
    lcp.wait_send()
    for t in range(2):
        core_copy(t).wait_send()
        ca_copy(t).wait_send()


def body(embeddings, fine_labels, prototypes, coarse_protos, coarse_labels):
    vmem = pl.BlockSpec(memory_space=pltpu.VMEM)
    sem = pltpu.SemaphoreType.DMA
    scratch = [
        pltpu.VMEM((G, ROWS, D), BF16),
        pltpu.VMEM((G, 1, ROWS), jnp.int32),
        pltpu.VMEM((ROWS, D), F32),
        pltpu.VMEM((ROWS, 128), F32),
        pltpu.VMEM((D, KL), BF16),
        pltpu.VMEM((D, KC), BF16),
        pltpu.VMEM((KL, ROWS), F32),
        pltpu.VMEM((KL, ROWS), F32),
        pltpu.VMEM((G, KL, ROWS), BF16),
        pltpu.VMEM((G, D, ROWS), F32),
        pltpu.VMEM((G, D, ROWS), BF16),
        pltpu.VMEM((G, ROWS, D), BF16),
        pltpu.VMEM((G, D, ROWS), BF16),
        pltpu.VMEM((G, D, ROWS), BF16),
        pltpu.VMEM((D, ROWS), F32),
        pltpu.VMEM((KL, D), F32),
        pltpu.VMEM((KL, D), F32),
        pltpu.VMEM((KC, D), F32),
        pltpu.VMEM((D, KL), F32),
        pltpu.VMEM((KL, D), F32),
        pltpu.VMEM((G, 16, ROWS), F32),
        pltpu.VMEM((G, 4, ROWS), F32),
        pltpu.VMEM((G, ROWS), F32),
        pltpu.VMEM((4, 4, ROWS), F32),
        pltpu.VMEM((G, ROWS), F32),
        pltpu.VMEM((G, 8, 128), F32),
        pltpu.VMEM((G, 8, 128), F32),
        pltpu.VMEM((G, 8, 128), F32),
        pltpu.VMEM((2, 8, 64, D), BF16),
        pltpu.VMEM((2, 8, 64, D), BF16),
        pltpu.VMEM((2, 2, 8, 64, D), BF16),
        pltpu.VMEM((2, 8, 64, D), BF16),
        pltpu.VMEM((2, 2, 8, 64, D), BF16),
        pltpu.VMEM((G, 8, 128), F32),
        pltpu.VMEM((2, 8, 128), F32),
        pltpu.VMEM((8, 8, 128), F32),
        sem((N_GATHER,)), sem((N_GATHER,)),
        sem((G,)), sem((G,)), sem((G,)), sem((G,)), sem((G,)), sem((G,)),
        sem((8,)), sem((8,)),
        sem((G,)), sem((G,)), sem((G,)), sem((G,)), sem((G,)), sem((G,)), sem((G,)), sem((G,)),
        sem((2,)), sem((2,)),
        sem((2, 8)), sem((2, 8)), sem((2, 8)), sem((2, 8)),
        sem((2,)), sem((2,)),
        sem((8,)), sem((8,)),
    ]
    outs = [
        pltpu.VMEM((ROWS, D), F32),
        pltpu.VMEM((KL, D), F32),
        pltpu.VMEM((KL, D), F32),
        pltpu.VMEM((KC, D), F32),
        jax.ShapeDtypeStruct((1, 1), F32),
    ]
    ge, gp, new, gc, loss = pl.pallas_call(
        kernel,
        out_shape=outs,
        in_specs=[vmem] * 5,
        out_specs=[vmem] * 5,
        scratch_shapes=scratch,
        compiler_params=pltpu.CompilerParams(
            collective_id=0, has_side_effects=True, vmem_limit_bytes=56 * 1024 * 1024
        ),
    )(embeddings, fine_labels.reshape(1, ROWS), prototypes, coarse_protos, coarse_labels.reshape(1, KC))
    return ge, gp, new, gc, loss.reshape(())


def solution(mesh):
    in_specs = (P(("rows", "group"), None), P(("rows", "group")), P("group", None), P(), P("group"))
    out_specs = (P(("rows", "group"), None), P("group", None), P("group", None), P(), P())
    return jax.shard_map(body, mesh=mesh, in_specs=in_specs, out_specs=out_specs, check_vma=False)
```

time: 102 us -> 79.4 us (0.78)
  the two profiles are of different devices: /device:TPU:31 before, /device:TPU:1 now
where the time goes in v2:
time: 79.4 us; the launch traced here: 79.3 us
  Pallas kernels  73.3 us (92%)
  local copies, waits for them, and re-layouts  3.61 us (5%)
  between operations  2.33 us (3%)
    pallas_call x1, Pallas kernels, body(): pl.pallas_call(kernel, out_shape=outs, in_specs=[vmem] * 5, out_specs=[vm...  73.3 us
    unnamed x4, local copies, waits for them, and re-layouts  3.61 us

profile of v2, /device:TPU:1, one launch (start us, length us, event | category | flops | bytes accessed | tf_op | source)
XLA Modules:
  0.0 79.3 jit_solution(7820135818596127951)
XLA Ops:
  0.6 73.3 %shard_map.92 = (f32[256,256]{1,0:T(8,128)S(1)}, f32[1024,256]{1,0:T(8,128)S(1)}, f32[1024,256]{1,0:T(8,128)S(1)}, f32[1024,256]{1,0:T(8,128)S(1)}, f32[1,1]{1,0:T(1,128)}) custom-call(bf16[256,256]{1,0:T(8,128)(2,1)} %emb.1, s32[1,256]{1,0:T(1,128)} %bitcast.4, bf16[1024,256]{1,0:T(8,128)(2,1)} %protos.1, bf16[1024,256]{1,0:T(8,128)(2,1)} %coarse.1, ...), custom_call_target="tpu_custom_call" | custom-call | tf_op jit(solution)/shard_map/pallas_call | solution.py:572
  73.9 0.7 copy.15
  74.7 1.0 %copy.16 = f32[1024,256]{1,0:T(8,128)} copy(f32[1024,256]{1,0:T(8,128)S(1)} %get-tuple-element.16) | data formatting | bytes 2097152
  75.6 1.0 %copy.17 = f32[1024,256]{1,0:T(8,128)} copy(f32[1024,256]{1,0:T(8,128)S(1)} %get-tuple-element.17) | data formatting | bytes 2097152
  76.6 1.0 %copy.18 = f32[1024,256]{1,0:T(8,128)} copy(f32[1024,256]{1,0:T(8,128)S(1)} %get-tuple-element.18) | data formatting | bytes 2097152

commit v3 on v2

--- a/solution.py
+++ b/solution.py
@@ -52,8 +52,8 @@
     o_emb, o_pg, o_new, o_cg, o_loss,
     gbuf, labs, unit_s, inv_s, protos_t, coarse_t, lscr, lscr2, ebuf, obuf, lbuf, us, rout, rin, own_rt,
     mem, soft, cg, cpart_t, cpart, stats_a, stats_b, mmax, lt_a, wbuf,
-    cg_out, cg_in, cg_all, cg_fin, core_in, z_out, z_in, fin, extra, loss_core, loss_z,
-    gs, gr, labs_s, labs_r, cgo_s, cgo_r, cga_s, cga_r, cgz_s, cgz_r, sa_s, sa_r, sb_s, sb_r, ex_s, ex_r,
+    cg_out, cg_in, cg_all, cg_fin, core_in, z_out, z_in, fin, loss_core, loss_z,
+    gs, gr, labs_s, labs_r, cgo_s, cgo_r, cga_s, cga_r, cgz_s, cgz_r, sa_s, sa_r, sb_s, sb_r,
     rw_s, rw_r, co_s, co_r, zo_s, zo_r, za_s, za_r, ca_s, ca_r, ls_s, ls_r,
 ):
     r = lax.axis_index("rows")
@@ -215,6 +215,14 @@
         else:
             stats_a[0, pl.ds(SLOT[dx] * 4 + ys[dy], 1), :] = lse
 
+    def label_rows(*which):
+        for k in which:
+            labels = local_labels(ORDER[k])
+            out = None
+            for j, rows in enumerate(parts):
+                out = add(out, dot(protos_t[:, rows], onehot(labels, j)))
+            lbuf[k] = out.astype(BF16)
+
     coarse_loss = coarse_block(0)
     first_pass(0, None)
 
@@ -281,6 +289,7 @@
         cp.start()
         cga_x.append(cp)
 
+    label_rows(0, 1, 2)
     arrived(a3f, b3f, a4f, b4f)
     first_pass(9, 8)
     arrived(p1f, p2f, p3f, p4f)
@@ -288,6 +297,7 @@
     first_pass(11, 10)
     sa_x = exchange(lambda k: stats_a.at[0], lambda s: stats_a.at[s], sa_s, sa_r)
     first_pass(12, 11)
+    label_rows(3, 4, 5)
     arrived(q1f, q2f, q3f, q4f)
     first_pass(13, 12)
     first_pass(14, 13)
@@ -306,8 +316,12 @@
     for d in range(1, 8):
         cgz_copy(d).start()
 
+    label_rows(6, 7, 8, 9)
     arrived(p5f, q5f, p6f, q6f)
     first_pass(15, 14)
+    target = 10.0 * total(mem[...] * protos[...].astype(F32))
+    head = lax.broadcasted_iota(jnp.int32, (4, ROWS), 0) == 0
+    stats_b[0, 4:8, :] = jnp.where(head, target, coarse_loss)
     sb_x = exchange(lambda k: stats_b.at[0], lambda s: stats_b.at[s], sb_s, sb_r)
 
     @functools.cache
@@ -369,24 +383,13 @@
         ca_copy(t).start()
 
     core_send(0, mem)
-    target = 10.0 * total(mem[...] * protos[...].astype(F32))
-    first = lax.broadcasted_iota(jnp.int32, (8, 128), 0) == 0
-    extra[0] = jnp.where(first, target, coarse_loss)
-    ex_x = exchange(lambda k: extra.at[0], lambda s: extra.at[s], ex_s, ex_r)
     core_merge(0, mem)
 
     last = None
     for rows in parts:
         last = add(last, dot(protos_t[:, rows], ebuf[15, rows, :]))
     obuf[15] = last
-    for k, p in enumerate(ORDER):
-        labels = local_labels(p)
-        out = None
-        for j, rows in enumerate(parts):
-            out = add(out, dot(protos_t[:, rows], onehot(labels, j)))
-        lbuf[k] = out.astype(BF16)
-    for rows in parts:
-        cpart[rows, :] = cpart_t[:, rows].T
+    label_rows(10, 11, 12, 13, 14, 15)
 
     arrived(*sa_x)
     arrived(*sb_x)
@@ -394,7 +397,7 @@
     def line(a, b, dx):
         away = (dx - a) % 4
         if away == 2:
-            return stats_b[rel(a, b)]
+            return stats_b[rel(a, b), 0:4, :]
         return stats_a[rel(a, b), SLOT[away] * 4 : SLOT[away] * 4 + 4, :]
 
     loss_rows = None
@@ -418,7 +421,7 @@
             rout.at[k], rin.at[k], rw_s.at[k], rw_r.at[k], device_id=plane(*p), device_id_type=MESH
         )
         cp.start()
-        rw_x.append(cp)
+        rw_x.append((cp, k))
     own_rt[...] = row_terms(0)
 
     for j, rows in enumerate(parts):
@@ -432,8 +435,7 @@
         soft[rows, :] = acc
 
     core_send(1, soft)
-    arrived(*ex_x)
-    sums = functools.reduce(add, [extra[k] for k in range(G)])
+    sums = functools.reduce(add, [stats_b[k, 4:8, :] for k in range(G)])
     coarse_all = sums[1:2, 0:1]
     loss_core[0] = jnp.broadcast_to(total(loss_rows) - sums[0:1, 0:1], (8, 128))
     lcp = pltpu.make_async_remote_copy(
@@ -453,6 +455,8 @@
     for d in range(1, 8):
         lz_copy(d).start()
 
+    for rows in parts:
+        cpart[rows, :] = cpart_t[:, rows].T
     for d in range(1, 8):
         cgz_copy(d).wait_recv()
 
@@ -475,42 +479,52 @@
         o_new[rows, :] = 0.5 * p32 + (0.5 * norm) * (members * length)
         cpart[rows, :] = cpart[rows, :] - 2.5 * members
 
-    arrived(*rw_x)
+    z_gathered(1)
+
+    half = (G - 1) // 2
     acc = own_rt[...]
-    for k in range(1, G):
+    for cp, k in rw_x[:half]:
+        cp.wait_recv()
+        acc = acc + rin[k].astype(F32)
+    own_rt[...] = acc
+    for cp in gathers + lab_x + cgo_x + cga_x + sa_x + sb_x:
+        cp.wait_send()
+    for d in range(1, 8):
+        cgz_copy(d).wait_send()
+        for t in range(2):
+            z_copy(t, d).wait_send()
+    core_copy(0).wait_send()
+    core_copy(1).wait_send()
+    lcp.wait_send()
+    for d in range(1, 8):
+        za_copy(0, d).wait_send()
+    cgc.wait_send()
+    ca_copy(0).wait_send()
+
+    for d in range(1, 8):
+        lz_copy(d).wait_recv()
+    fine = functools.reduce(add, [loss_z[d] for d in range(8)])
+    o_loss[...] = fine[0:1, 0:1] * (1.0 / (G * G * ROWS)) + coarse_all * (1.0 / (KL * G))
+
+    ca_copy(1).wait_recv()
+    for j, rows in enumerate(parts):
+        part = fin[1, j // 2, (j % 2) * 4 : (j % 2) * 4 + 4].reshape(256, D).astype(F32)
+        o_pg[rows, :] = cpart[rows, :] + 2.5 * part
+    for d in range(1, 8):
+        lz_copy(d).wait_send()
+        za_copy(1, d).wait_send()
+    ca_copy(1).wait_send()
+
+    acc = own_rt[...]
+    for cp, k in rw_x[half:]:
+        cp.wait_recv()
         acc = acc + rin[k].astype(F32)
     row_grad = acc.T
     unit = unit_s[...]
     inv = inv_s[:, 0:1]
     o_emb[...] = inv * (row_grad - unit * jnp.sum(unit * row_grad, axis=1, keepdims=True))
-
-    for d in range(1, 8):
-        lz_copy(d).wait_recv()
-
-    fine = functools.reduce(add, [loss_z[d] for d in range(8)])
-    o_loss[...] = fine[0:1, 0:1] * (1.0 / (G * G * ROWS)) + coarse_all * (1.0 / (KL * G))
-
-    z_gathered(1)
-    ca_copy(1).wait_recv()
-    for j, rows in enumerate(parts):
-        part = fin[1, j // 2, (j % 2) * 4 : (j % 2) * 4 + 4].reshape(256, D).astype(F32)
-        o_pg[rows, :] = cpart[rows, :] + 2.5 * part
-
-    for cp in gathers + lab_x + cgo_x + cga_x + sa_x + sb_x + ex_x + rw_x:
+    for cp, _ in rw_x:
         cp.wait_send()
-
-    for d in range(1, 8):
-        cgz_copy(d).wait_send()
-        lz_copy(d).wait_send()
-        for t in range(2):
-            z_copy(t, d).wait_send()
-            za_copy(t, d).wait_send()
-
-    cgc.wait_send()
-    lcp.wait_send()
-    for t in range(2):
-        core_copy(t).wait_send()
-        ca_copy(t).wait_send()
 
 
 def body(embeddings, fine_labels, prototypes, coarse_protos, coarse_labels):
@@ -538,7 +552,7 @@
         pltpu.VMEM((D, KL), F32),
         pltpu.VMEM((KL, D), F32),
         pltpu.VMEM((G, 16, ROWS), F32),
-        pltpu.VMEM((G, 4, ROWS), F32),
+        pltpu.VMEM((G, 8, ROWS), F32),
         pltpu.VMEM((G, ROWS), F32),
         pltpu.VMEM((4, 4, ROWS), F32),
         pltpu.VMEM((G, ROWS), F32),
@@ -550,13 +564,12 @@
         pltpu.VMEM((2, 2, 8, 64, D), BF16),
         pltpu.VMEM((2, 8, 64, D), BF16),
         pltpu.VMEM((2, 2, 8, 64, D), BF16),
-        pltpu.VMEM((G, 8, 128), F32),
         pltpu.VMEM((2, 8, 128), F32),
         pltpu.VMEM((8, 8, 128), F32),
         sem((N_GATHER,)), sem((N_GATHER,)),
         sem((G,)), sem((G,)), sem((G,)), sem((G,)), sem((G,)), sem((G,)),
         sem((8,)), sem((8,)),
-        sem((G,)), sem((G,)), sem((G,)), sem((G,)), sem((G,)), sem((G,)), sem((G,)), sem((G,)),
+        sem((G,)), sem((G,)), sem((G,)), sem((G,)), sem((G,)), sem((G,)),
         sem((2,)), sem((2,)),
         sem((2, 8)), sem((2, 8)), sem((2, 8)), sem((2, 8)),
         sem((2,)), sem((2,)),

time: 79.4 us -> 77 us (0.970)
  Pallas kernels: 73.3 us -> 70.9 us
    pallas_call x1, Pallas kernels: 73.3 us -> 70.9 us  [body(): pl.pallas_call(kernel, out_shape=outs, in_specs=[vmem] * 5, out_specs=[vm...]
where the time goes in v3:
time: 77 us; the launch traced here: 76.9 us
  Pallas kernels  70.9 us (92%)
  local copies, waits for them, and re-layouts  3.61 us (5%)
  between operations  2.33 us (3%)
    pallas_call x1, Pallas kernels, body(): pl.pallas_call(kernel, out_shape=outs, in_specs=[vmem] * 5, out_specs=[vm...  70.9 us
    unnamed x4, local copies, waits for them, and re-layouts  3.61 us

profile of v3, /device:TPU:1, one launch (start us, length us, event | category | flops | bytes accessed | tf_op | source)
XLA Modules:
  0.0 76.9 jit_solution(13868254076720352883)
XLA Ops:
  0.6 70.9 %shard_map.92 = (f32[256,256]{1,0:T(8,128)S(1)}, f32[1024,256]{1,0:T(8,128)S(1)}, f32[1024,256]{1,0:T(8,128)S(1)}, f32[1024,256]{1,0:T(8,128)S(1)}, f32[1,1]{1,0:T(1,128)}) custom-call(bf16[256,256]{1,0:T(8,128)(2,1)} %emb.1, s32[1,256]{1,0:T(1,128)} %bitcast.4, bf16[1024,256]{1,0:T(8,128)(2,1)} %protos.1, bf16[1024,256]{1,0:T(8,128)(2,1)} %coarse.1, ...), custom_call_target="tpu_custom_call" | custom-call | tf_op jit(solution)/shard_map/pallas_call | solution.py:585
  71.5 0.7 copy.15
  72.3 1.0 %copy.16 = f32[1024,256]{1,0:T(8,128)} copy(f32[1024,256]{1,0:T(8,128)S(1)} %get-tuple-element.16) | data formatting | bytes 2097152
  73.2 1.0 %copy.17 = f32[1024,256]{1,0:T(8,128)} copy(f32[1024,256]{1,0:T(8,128)S(1)} %get-tuple-element.17) | data formatting | bytes 2097152
  74.2 1.0 %copy.18 = f32[1024,256]{1,0:T(8,128)} copy(f32[1024,256]{1,0:T(8,128)S(1)} %get-tuple-element.18) | data formatting | bytes 2097152

commit v4 on v3

--- a/solution.py
+++ b/solution.py
@@ -44,6 +44,8 @@
 ORDER = [(0, 0), (1, 0), (3, 0), (0, 1), (0, 3), (1, 1), (1, 3), (3, 1), (3, 3), (0, 2), (1, 2), (3, 2)]
 ORDER += [(2, 0), (2, 1), (2, 3), (2, 2)]
 PEERS = ORDER[1:]
+ROW_ORDER = [(2, 2), (2, 1), (1, 2), (2, 3), (3, 2), (2, 0), (0, 2), (1, 1), (3, 3), (1, 3), (3, 1)]
+ROW_ORDER += [(1, 0), (0, 1), (3, 0), (0, 3)]
 SLOT = {0: 0, 1: 1, 3: 2}
 
 
@@ -52,8 +54,8 @@
     o_emb, o_pg, o_new, o_cg, o_loss,
     gbuf, labs, unit_s, inv_s, protos_t, coarse_t, lscr, lscr2, ebuf, obuf, lbuf, us, rout, rin, own_rt,
     mem, soft, cg, cpart_t, cpart, stats_a, stats_b, mmax, lt_a, wbuf,
-    cg_out, cg_in, cg_all, cg_fin, core_in, z_out, z_in, fin, loss_core, loss_z,
-    gs, gr, labs_s, labs_r, cgo_s, cgo_r, cga_s, cga_r, cgz_s, cgz_r, sa_s, sa_r, sb_s, sb_r,
+    cg_x, cg_y, cg_fin, core_in, z_out, z_in, fin, loss_core, loss_z,
+    gs, gr, labs_s, labs_r, cgx_s, cgx_r, cgy_s, cgy_r, cga_s, cga_r, cgz_s, cgz_r, sa_s, sa_r, sb_s, sb_r,
     rw_s, rw_r, co_s, co_r, zo_s, zo_r, za_s, za_r, ca_s, ca_r, ls_s, ls_r,
 ):
     r = lax.axis_index("rows")
@@ -245,19 +247,21 @@
 
     base = c * 512 + z * 64
 
-    def tile_of(q):
-        return cg[pl.ds(pl.multiple_of(base + 8 * (q // 2), 8), 8), (q % 2) * 128 : (q % 2) * 128 + 128]
-
-    for q in range(G):
-        cg_out[q] = tile_of(q)
-    cgo_x = []
-    for k, p in enumerate(PEERS):
-        cp = pltpu.make_async_remote_copy(
-            cg_out.at[xs[p[0]] + ys[p[1]]], cg_in.at[k], cgo_s.at[k], cgo_r.at[k],
-            device_id=plane(*p), device_id_type=MESH,
-        )
-        cp.start()
-        cgo_x.append(cp)
+    def slice_of(at):
+        return cg.at[pl.ds(pl.multiple_of(base + 16 * at, 16), 16), :]
+
+    def line_copies(src, dst, send_sem, recv_sem, target):
+        copies = []
+        for d in (2, 1, 3):
+            cp = pltpu.make_async_remote_copy(
+                src(d), dst, send_sem.at[d], recv_sem.at[d], device_id=target(d), device_id_type=MESH
+            )
+            cp.start()
+            copies.append(cp)
+        return copies
+
+    cgx_c = line_copies(lambda d: slice_of(lax.rem(x + d, 4)), cg_x.at[x], cgx_s, cgx_r, lambda d: plane(d, 0))
+    cg_x[x] = slice_of(x)[...]
 
     arrived(*lab_x)
     arrived(f1, f2)
@@ -273,27 +277,22 @@
     first_pass(5, 4)
     p5f, q5f, p6f, q6f = on_y(p5, 2, True), on_x(q5, 2, True), on_y(p6, 2, False), on_x(q6, 2, False)
     first_pass(6, 5)
+    arrived(*cgx_c)
+    cg_y[y] = cg_x[0] + cg_x[1] + cg_x[2] + cg_x[3]
+    cgy_c = line_copies(lambda d: cg_y.at[y], cg_y.at[y], cgy_s, cgy_r, lambda d: plane(0, d))
     first_pass(7, 6)
     first_pass(8, 7)
-
-    arrived(*cgo_x)
-    tile = cg_out[g]
-    for k in range(G - 1):
-        tile = tile + cg_in[k]
-    cg_all[g] = (KC / (KL * G)) * tile
-    cga_x = []
-    for k, p in enumerate(PEERS):
-        cp = pltpu.make_async_remote_copy(
-            cg_all.at[g], cg_all.at[g], cga_s.at[k], cga_r.at[k], device_id=plane(*p), device_id_type=MESH
-        )
-        cp.start()
-        cga_x.append(cp)
-
     label_rows(0, 1, 2)
     arrived(a3f, b3f, a4f, b4f)
     first_pass(9, 8)
     arrived(p1f, p2f, p3f, p4f)
     first_pass(10, 9)
+    arrived(*cgy_c)
+    tile = (KC / (KL * G)) * (cg_y[0] + cg_y[1] + cg_y[2] + cg_y[3])
+    own_rows = pl.ds(pl.multiple_of(16 * x, 16), 16)
+    cg_fin[c, z, own_rows, :] = tile.astype(BF16)
+    cg_part = cg_fin.at[c, z, own_rows]
+    cga_c = line_copies(lambda d: cg_part, cg_part, cga_s, cga_r, lambda d: plane(d, 0))
     first_pass(11, 10)
     sa_x = exchange(lambda k: stats_a.at[0], lambda s: stats_a.at[s], sa_s, sa_r)
     first_pass(12, 11)
@@ -302,9 +301,7 @@
     first_pass(13, 12)
     first_pass(14, 13)
 
-    arrived(*cga_x)
-    for q in range(G):
-        cg_fin[c, z, (q // 2) * 8 : (q // 2) * 8 + 8, (q % 2) * 128 : (q % 2) * 128 + 128] = cg_all[q].astype(BF16)
+    arrived(*cga_c)
 
     @functools.cache
     def cgz_copy(d):
@@ -383,13 +380,13 @@
         ca_copy(t).start()
 
     core_send(0, mem)
-    core_merge(0, mem)
 
     last = None
     for rows in parts:
         last = add(last, dot(protos_t[:, rows], ebuf[15, rows, :]))
     obuf[15] = last
     label_rows(10, 11, 12, 13, 14, 15)
+    core_merge(0, mem)
 
     arrived(*sa_x)
     arrived(*sb_x)
@@ -414,16 +411,14 @@
         return 10.0 * (obuf[k] * wbuf[k : k + 1, :] - lbuf[k].astype(F32))
 
     rw_x = []
-    for k in range(G - 1, 0, -1):
-        p = ORDER[k]
+    for p in ROW_ORDER:
+        k = ORDER.index(p)
         rout[k] = row_terms(k).astype(BF16)
         cp = pltpu.make_async_remote_copy(
             rout.at[k], rin.at[k], rw_s.at[k], rw_r.at[k], device_id=plane(*p), device_id_type=MESH
         )
         cp.start()
         rw_x.append((cp, k))
-    own_rt[...] = row_terms(0)
-
     for j, rows in enumerate(parts):
         acc = None
         for k, p in enumerate(ORDER):
@@ -435,6 +430,7 @@
         soft[rows, :] = acc
 
     core_send(1, soft)
+    own_rt[...] = row_terms(0)
     sums = functools.reduce(add, [stats_b[k, 4:8, :] for k in range(G)])
     coarse_all = sums[1:2, 0:1]
     loss_core[0] = jnp.broadcast_to(total(loss_rows) - sums[0:1, 0:1], (8, 128))
@@ -487,7 +483,7 @@
         cp.wait_recv()
         acc = acc + rin[k].astype(F32)
     own_rt[...] = acc
-    for cp in gathers + lab_x + cgo_x + cga_x + sa_x + sb_x:
+    for cp in gathers + lab_x + cgx_c + cgy_c + cga_c + sa_x + sb_x:
         cp.wait_send()
     for d in range(1, 8):
         cgz_copy(d).wait_send()
@@ -556,9 +552,8 @@
         pltpu.VMEM((G, ROWS), F32),
         pltpu.VMEM((4, 4, ROWS), F32),
         pltpu.VMEM((G, ROWS), F32),
-        pltpu.VMEM((G, 8, 128), F32),
-        pltpu.VMEM((G, 8, 128), F32),
-        pltpu.VMEM((G, 8, 128), F32),
+        pltpu.VMEM((4, 16, D), F32),
+        pltpu.VMEM((4, 16, D), F32),
         pltpu.VMEM((2, 8, 64, D), BF16),
         pltpu.VMEM((2, 8, 64, D), BF16),
         pltpu.VMEM((2, 2, 8, 64, D), BF16),
@@ -567,7 +562,7 @@
         pltpu.VMEM((2, 8, 128), F32),
         pltpu.VMEM((8, 8, 128), F32),
         sem((N_GATHER,)), sem((N_GATHER,)),
-        sem((G,)), sem((G,)), sem((G,)), sem((G,)), sem((G,)), sem((G,)),
+        sem((G,)), sem((G,)), sem((4,)), sem((4,)), sem((4,)), sem((4,)), sem((4,)), sem((4,)),
         sem((8,)), sem((8,)),
         sem((G,)), sem((G,)), sem((G,)), sem((G,)), sem((G,)), sem((G,)),
         sem((2,)), sem((2,)),

time: 77 us -> 76.3 us (level)
  no operation moved by 1% of the time
where the time goes in v4:
time: 76.3 us; the launch traced here: 76.2 us
  Pallas kernels  70.2 us (92%)
  local copies, waits for them, and re-layouts  3.61 us (5%)
  between operations  2.33 us (3%)
    pallas_call x1, Pallas kernels, body(): pl.pallas_call(kernel, out_shape=outs, in_specs=[vmem] * 5, out_specs=[vm...  70.2 us
    unnamed x4, local copies, waits for them, and re-layouts  3.61 us

profile of v4, /device:TPU:1, one launch (start us, length us, event | category | flops | bytes accessed | tf_op | source)
XLA Modules:
  0.0 76.2 jit_solution(1789731162555190776)
XLA Ops:
  0.6 70.2 %shard_map.92 = (f32[256,256]{1,0:T(8,128)S(1)}, f32[1024,256]{1,0:T(8,128)S(1)}, f32[1024,256]{1,0:T(8,128)S(1)}, f32[1024,256]{1,0:T(8,128)S(1)}, f32[1,1]{1,0:T(1,128)}) custom-call(bf16[256,256]{1,0:T(8,128)(2,1)} %emb.1, s32[1,256]{1,0:T(1,128)} %bitcast.4, bf16[1024,256]{1,0:T(8,128)(2,1)} %protos.1, bf16[1024,256]{1,0:T(8,128)(2,1)} %coarse.1, ...), custom_call_target="tpu_custom_call" | custom-call | tf_op jit(solution)/shard_map/pallas_call | solution.py:580
  70.9 0.7 copy.15
  71.6 1.0 %copy.16 = f32[1024,256]{1,0:T(8,128)} copy(f32[1024,256]{1,0:T(8,128)S(1)} %get-tuple-element.16) | data formatting | bytes 2097152
  72.5 1.0 %copy.17 = f32[1024,256]{1,0:T(8,128)} copy(f32[1024,256]{1,0:T(8,128)S(1)} %get-tuple-element.17) | data formatting | bytes 2097152
  73.5 1.0 %copy.18 = f32[1024,256]{1,0:T(8,128)} copy(f32[1024,256]{1,0:T(8,128)S(1)} %get-tuple-element.18) | data formatting | bytes 2097152

commit v5 on v4

--- a/solution.py
+++ b/solution.py
@@ -243,6 +243,10 @@
     coarse_loss = coarse_loss + coarse_block(1)
     a3f, b3f, a4f, b4f = on_y(a3, 0, True), on_x(b3, 0, True), on_y(a4, 0, False), on_x(b4, 0, False)
     coarse_loss = coarse_loss + coarse_block(2)
+    arrived(f1, f2)
+    p5, p6 = both_y(2, 0)
+    arrived(g1, g2)
+    q5, q6 = both_x(0, 2)
     coarse_loss = coarse_loss + coarse_block(3)
 
     base = c * 512 + z * 64
@@ -264,18 +268,14 @@
     cg_x[x] = slice_of(x)[...]
 
     arrived(*lab_x)
-    arrived(f1, f2)
-    p5, p6 = both_y(2, 0)
-    arrived(g1, g2)
-    q5, q6 = both_x(0, 2)
     first_pass(1, 0)
+    p1f, q1f, p2f, q2f = on_y(p1, 3, True), on_x(q1, 3, True), on_y(p2, 3, False), on_x(q2, 3, False)
     first_pass(2, 1)
-    p1f, q1f, p2f, q2f = on_y(p1, 3, True), on_x(q1, 3, True), on_y(p2, 3, False), on_x(q2, 3, False)
+    p3f, q3f, p4f, q4f = on_y(p3, 1, True), on_x(q3, 1, True), on_y(p4, 1, False), on_x(q4, 1, False)
     first_pass(3, 2)
-    p3f, q3f, p4f, q4f = on_y(p3, 1, True), on_x(q3, 1, True), on_y(p4, 1, False), on_x(q4, 1, False)
     first_pass(4, 3)
+    p5f, q5f, p6f, q6f = on_y(p5, 2, True), on_x(q5, 2, True), on_y(p6, 2, False), on_x(q6, 2, False)
     first_pass(5, 4)
-    p5f, q5f, p6f, q6f = on_y(p5, 2, True), on_x(q5, 2, True), on_y(p6, 2, False), on_x(q6, 2, False)
     first_pass(6, 5)
     arrived(*cgx_c)
     cg_y[y] = cg_x[0] + cg_x[1] + cg_x[2] + cg_x[3]

time: 76.3 us -> 77 us (level)
  no operation moved by 1% of the time
where the time goes in v5:
time: 77 us; the launch traced here: 76.9 us
  Pallas kernels  70.9 us (92%)
  local copies, waits for them, and re-layouts  3.61 us (5%)
  between operations  2.33 us (3%)
    pallas_call x1, Pallas kernels, body(): pl.pallas_call(kernel, out_shape=outs, in_specs=[vmem] * 5, out_specs=[vm...  70.9 us
    unnamed x4, local copies, waits for them, and re-layouts  3.61 us

profile of v5, /device:TPU:1, one launch (start us, length us, event | category | flops | bytes accessed | tf_op | source)
XLA Modules:
  0.0 76.9 jit_solution(4854489884766778271)
XLA Ops:
  0.6 70.9 %shard_map.92 = (f32[256,256]{1,0:T(8,128)S(1)}, f32[1024,256]{1,0:T(8,128)S(1)}, f32[1024,256]{1,0:T(8,128)S(1)}, f32[1024,256]{1,0:T(8,128)S(1)}, f32[1,1]{1,0:T(1,128)}) custom-call(bf16[256,256]{1,0:T(8,128)(2,1)} %emb.1, s32[1,256]{1,0:T(1,128)} %bitcast.4, bf16[1024,256]{1,0:T(8,128)(2,1)} %protos.1, bf16[1024,256]{1,0:T(8,128)(2,1)} %coarse.1, ...), custom_call_target="tpu_custom_call" | custom-call | tf_op jit(solution)/shard_map/pallas_call | solution.py:580
  71.6 0.7 copy.15
  72.3 1.0 %copy.16 = f32[1024,256]{1,0:T(8,128)} copy(f32[1024,256]{1,0:T(8,128)S(1)} %get-tuple-element.16) | data formatting | bytes 2097152
  73.2 1.0 %copy.17 = f32[1024,256]{1,0:T(8,128)} copy(f32[1024,256]{1,0:T(8,128)S(1)} %get-tuple-element.17) | data formatting | bytes 2097152
  74.2 1.0 %copy.18 = f32[1024,256]{1,0:T(8,128)} copy(f32[1024,256]{1,0:T(8,128)S(1)} %get-tuple-element.18) | data formatting | bytes 2097152
